TPU v7x, 512 devices: a whole 4x4x16 slice. The times are simulated.
512 devices in a mesh: pipe: 32 (over z, core), ulysses: 4 (over x), rep: 4 (over y).
Axes of the slice: x: 4, y: 4, z: 16, core: 2. Of those that a mesh axis runs over, the one named last changes fastest.
Arguments:
- latent: float32 [48, 32, 64], P('rep'), parts along dimension 0, may hold values from -6 to 6
- timesteps: int32 [8], P('rep'), parts along dimension 0, may hold values from 1 to 1000
- w_in: bfloat16 [64, 1536], replicated, may hold values from -0.75 to 0.75
- w_out: bfloat16 [1536, 64], replicated, may hold values from -0.15625 to 0.15625
- out_gain: float32 [1536], replicated, may hold values from 0.5 to 1.5
- w_qkv: bfloat16 [32, 1536, 12, 3, 128], P('pipe', None, 'ulysses'), may hold values from -0.15625 to 0.15625
- norm_gain: float32 [32, 1536], P('pipe'), may hold values from 0.5 to 1.5
- modulation: float32 [32, 1536], P('pipe'), may hold values from -3 to 3
- q_gain: float32 [32, 128], P('pipe'), may hold values from 0.5 to 1.5
- k_gain: float32 [32, 128], P('pipe'), may hold values from 0.5 to 1.5
Outputs:
- caches: bfloat16 [32, 2, 1536, 1536], P('pipe', None, 'rep', 'ulysses'), parts along dimension 2
There are 4 independent parts, one for each index of `rep`. A program takes and returns all parts, laid end to end along the dimension named above; an argument that names none is the same for every part. Nothing has to cross between parts.
All inputs are finite; a program needn't handle non-finite values.
Results may differ from a plain program's by a relative error of at most 0.017.
Values may be sent and summed in bfloat16 or wider, within the bound.
A program may use at most 64 MiB of HBM per device.

v0:
```python
import jax
import jax.numpy as jnp
from jax import lax
from jax.sharding import PartitionSpec as P

EPS = 1e-06


def passed_along(block, axis, distance):
    devices = range(lax.axis_size(axis))
    route = [((i - distance) % len(devices), i) for i in devices]
    return lax.ppermute(block, axis, route)


def rms_scale(values):
    return values * lax.rsqrt(jnp.mean(values * values, axis=-1, keepdims=True) + EPS)


def head_norms(raw, q_scale, k_scale):
    query_rows = rms_scale(raw[:, :, 0]) * q_scale
    key = rms_scale(raw[:, :, 1]) * k_scale
    return jnp.stack([query_rows, key, raw[:, :, 2]], axis=2).astype(jnp.bfloat16)


def attend(query_rows, cached_key_rows, cached_value_rows, patch, step, patch_tok):
    score_scale = query_rows.shape[-1] ** (-0.5)
    attention_scores = (
        jnp.einsum("qkj,fkj->kqf", query_rows, cached_key_rows, preferred_element_type=jnp.float32)
        * score_scale
    )
    key_patch = lax.broadcasted_iota(jnp.int32, (cached_key_rows.shape[0],), 0) // patch_tok
    allowed = (key_patch <= patch) | (step > 0)
    attention_scores = jnp.where(allowed[None, None, :], attention_scores, jnp.float32(-1e30))
    softmax_weights = jnp.exp(attention_scores)
    softmax_weights = (softmax_weights / jnp.sum(softmax_weights, axis=-1, keepdims=True)).astype(
        jnp.bfloat16
    )
    attended_values = jnp.einsum(
        "bnf,fbv->nbv", softmax_weights, cached_value_rows, preferred_element_type=jnp.float32
    )
    return attended_values.astype(jnp.bfloat16)


def shards(latent, timesteps, w_in, w_out, out_gain, w_qkv, norm_gain, modulation, q_gain, k_gain):
    sections = lax.axis_size("pipe")
    section = lax.axis_index("pipe")
    groups = lax.axis_size("ulysses")
    member = lax.axis_index("ulysses")
    patches, patch_tok, channels = latent.shape
    part_rows = patch_tok // groups
    steps = timesteps.shape[0]
    width = w_in.shape[1]
    local_heads = w_qkv.shape[2]
    head_dim = w_qkv.shape[4]
    tokens = patches * patch_tok
    period = max(patches, sections)
    clocks = (steps - 1) * period + patches + sections - 1
    sigma = timesteps.astype(jnp.float32) / 1000.0
    weight_here = w_qkv[0]
    gain_here = norm_gain[0]
    shift_here = modulation[0]
    q_scale = q_gain[0]
    k_scale = k_gain[0]
    row_start = member * part_rows
    pending_init = lax.dynamic_slice_in_dim(latent, row_start, part_rows, 1)
    first = section == 0
    last = section == sections - 1

    def tick(clock, carry):
        hidden_out, latent_out, pending, cached_key_rows, cached_value_rows = carry
        hidden_in, latent_in = passed_along((hidden_out, latent_out), "pipe", 1)
        arrived = clock - sections
        arrived_step = jnp.floor_divide(arrived, period)
        arrived_patch = arrived - arrived_step * period
        stored = first & (arrived >= 0) & (arrived_patch < patches)
        slot = jnp.clip(arrived_patch, 0, patches - 1)
        pending = jnp.where(
            stored, lax.dynamic_update_index_in_dim(pending, latent_in, slot, 0), pending
        )
        job = clock - section
        step = jnp.floor_divide(job, period)
        patch = job - step * period
        active = (job >= 0) & (patch < patches) & (step < steps)
        patch_c = jnp.clip(patch, 0, patches - 1)
        step_c = jnp.clip(step, 0, steps - 1)
        latent_now = jnp.where(
            first, lax.dynamic_index_in_dim(pending, patch_c, 0, keepdims=False), latent_in
        )
        embedded = jnp.dot(
            latent_now.astype(jnp.bfloat16), w_in, preferred_element_type=jnp.float32
        )
        hidden = jnp.where(first, embedded, hidden_in)
        sigma_now = lax.dynamic_index_in_dim(sigma, step_c, 0, keepdims=False)
        normed = (rms_scale(hidden) * gain_here * (1.0 + sigma_now * shift_here)).astype(
            jnp.bfloat16
        )
        patch_in = lax.all_gather(normed, "ulysses", axis=0, tiled=True)

        def project_heads():
            raw = jnp.einsum(
                "rd,dhcn->rhcn", patch_in, weight_here, preferred_element_type=jnp.float32
            )
            return head_norms(raw, q_scale, k_scale)

        def empty_heads():
            return jnp.zeros((patch_tok, local_heads, 3, head_dim), jnp.bfloat16)

        qkv_rows = lax.cond(active, project_heads, empty_heads)

        def attend_patch(operands):
            qkv_now, key_store, value_store = operands
            start = patch_c * patch_tok
            key_store = lax.dynamic_update_slice_in_dim(key_store, qkv_now[:, :, 1], start, 0)
            value_store = lax.dynamic_update_slice_in_dim(value_store, qkv_now[:, :, 2], start, 0)
            attended_values = attend(
                qkv_now[:, :, 0], key_store, value_store, patch_c, step_c, patch_tok
            )
            return (
                attended_values.reshape(patch_tok, local_heads * head_dim),
                key_store,
                value_store,
            )

        def pass_patch(operands):
            return (
                jnp.zeros((patch_tok, local_heads * head_dim), jnp.bfloat16),
                operands[1],
                operands[2],
            )

        attended_values, cached_key_rows, cached_value_rows = lax.cond(
            active, attend_patch, pass_patch, (qkv_rows, cached_key_rows, cached_value_rows)
        )
        merged = lax.all_to_all(attended_values, "ulysses", split_axis=0, concat_axis=1, tiled=True)
        hidden_new = hidden + merged.astype(jnp.float32)
        final_normed = (rms_scale(hidden_new) * out_gain).astype(jnp.bfloat16)
        velocity = jnp.dot(final_normed, w_out, preferred_element_type=jnp.float32)
        step_next = jnp.minimum(step_c + 1, steps - 1)
        delta = lax.dynamic_index_in_dim(sigma, step_next, 0, keepdims=False) - sigma_now
        latent_new = jnp.where(last, latent_now + delta * velocity, latent_now)
        return (hidden_new, latent_new, pending, cached_key_rows, cached_value_rows)

    start_carry = (
        jnp.zeros((part_rows, width), jnp.float32),
        jnp.zeros((part_rows, channels), jnp.float32),
        pending_init,
        jnp.zeros((tokens, local_heads, head_dim), jnp.bfloat16),
        jnp.zeros((tokens, local_heads, head_dim), jnp.bfloat16),
    )
    result = lax.fori_loop(0, clocks, tick, start_carry)
    cached_key_rows, cached_value_rows = (result[3], result[4])
    stacked = jnp.stack([cached_key_rows, cached_value_rows], axis=0)
    return stacked.reshape(1, 2, tokens, local_heads * head_dim)


def solution(mesh):
    placed = (
        P("rep", None, None),
        P("rep"),
        P(),
        P(),
        P(),
        P("pipe", None, "ulysses", None, None),
        P("pipe", None),
        P("pipe", None),
        P("pipe", None),
        P("pipe", None),
    )
    return jax.shard_map(
        shards,
        mesh=mesh,
        in_specs=placed,
        out_specs=P("pipe", None, "rep", "ulysses"),
        check_vma=False,
    )
```

profile of v0, /device:TPU:505, one launch (start us, length us, event | category | flops | bytes accessed | tf_op | source)
XLA Modules:
  0.0 2199.6 jit_solution(13259621973974349579)
XLA Ops:
  1.6 2196.4 %while.25 = (s32[]{:T(128)}, f32[8,1536]{1,0:T(8,128)S(1)}, f32[8,64]{1,0:T(8,128)S(1)}, f32[12,8,64]{2,1,0:T(8,128)S(1)}, bf16[384,3,128]{2,0,1:T(8,128)(2,1)S(...) while((s32[]{:T(128)}, f32[8,1536]{1,0:T(8,128)S(1)}, ...), condition=%wide.region_10.11_spmd.clone, body=%wide.region_0.10_spmd.clone.sunk | while | flops 135818208 | bytes 7538575 | solution.py:150
  5.0 9.4 all_gather.13
  23.1 10.6 collective-permute-start.1
  37.0 9.0 all_gather.13
  54.5 10.3 collective-permute-start.1
  68.2 9.0 all_gather.13
  85.8 10.3 collective-permute-start.1
  99.4 9.0 all_gather.13
  117.0 10.3 collective-permute-start.1
  130.6 9.0 all_gather.13
  148.2 10.3 collective-permute-start.1
  161.8 9.0 all_gather.13
  179.4 10.3 collective-permute-start.1
  193.0 9.0 all_gather.13
  210.6 10.3 collective-permute-start.1
  224.3 9.0 all_gather.13
  241.8 10.3 collective-permute-start.1
  255.5 9.0 all_gather.13
  273.1 10.3 collective-permute-start.1
  286.7 9.0 all_gather.13
  304.3 10.3 collective-permute-start.1
  317.9 9.0 all_gather.13
  335.5 10.3 collective-permute-start.1
  349.1 9.0 all_gather.13
  366.7 10.3 collective-permute-start.1
  380.3 9.0 all_gather.13
  408.0 9.0 all_gather.13
  435.7 9.0 all_gather.13
  463.4 9.0 all_gather.13
  491.0 9.0 all_gather.13
  518.7 9.0 all_gather.13
  546.4 9.0 all_gather.13
  574.0 9.0 all_gather.13
  601.7 9.0 all_gather.13
  629.4 9.0 all_gather.13
  657.0 9.0 all_gather.13
  684.7 9.0 all_gather.13
  712.4 9.0 all_gather.13
  740.1 9.0 all_gather.13
  767.7 9.0 all_gather.13
  795.4 9.0 all_gather.13
  823.1 9.0 all_gather.13
  850.7 9.0 all_gather.13
  878.4 9.0 all_gather.13
  906.1 9.0 all_gather.13
  936.1 9.0 all_gather.13
  957.3 9.5 collective-permute-start.1
  970.1 9.0 all_gather.13
  1001.3 9.0 all_gather.13
  1032.5 9.0 all_gather.13
  1251.1 9.0 all_gather.13
  1299.9 10.3 collective-permute-start.1
  1313.6 9.0 all_gather.13
  1396.6 9.0 all_gather.13
  1479.6 9.0 all_gather.13
  1608.2 10.2 collective-permute-start.1
  1639.3 10.3 collective-permute-start.1
  1736.1 9.0 all_gather.13
  1763.8 9.0 all_gather.13
  1876.8 9.0 all_gather.13
  1906.8 9.0 all_gather.13
  1996.9 9.0 all_gather.13
  2026.9 9.0 all_gather.13
  2116.9 9.0 all_gather.13
  (2362 shorter events, 1640.3 us)
Async XLA Ops:
  15.0 7.7 all-to-all-start
  23.1 12.6 collective-permute-start.1
  54.5 12.3 collective-permute-start.1
  85.8 12.3 collective-permute-start.1
  117.0 12.3 collective-permute-start.1
  148.2 12.3 collective-permute-start.1
  179.4 12.3 collective-permute-start.1
  210.6 12.3 collective-permute-start.1
  241.8 12.3 collective-permute-start.1
  273.1 12.3 collective-permute-start.1
  304.3 12.3 collective-permute-start.1
  335.5 12.3 collective-permute-start.1
  366.7 12.3 collective-permute-start.1
  397.9 8.8 collective-permute-start.1
  425.6 8.8 collective-permute-start.1
  453.3 8.8 collective-permute-start.1
  480.9 8.8 collective-permute-start.1
  508.6 8.8 collective-permute-start.1
  536.3 8.8 collective-permute-start.1
  563.9 8.8 collective-permute-start.1
  591.6 8.8 collective-permute-start.1
  619.3 8.8 collective-permute-start.1
  647.0 8.8 collective-permute-start.1
  674.6 8.8 collective-permute-start.1
  702.3 8.8 collective-permute-start.1
  730.0 8.8 collective-permute-start.1
  757.6 8.8 collective-permute-start.1
  785.3 8.8 collective-permute-start.1
  813.0 8.8 collective-permute-start.1
  840.6 8.8 collective-permute-start.1
  868.3 8.8 collective-permute-start.1
  896.0 8.8 collective-permute-start.1
  957.3 11.5 collective-permute-start.1
  991.2 8.8 collective-permute-start.1
  1022.4 8.8 collective-permute-start.1
  1053.6 8.9 collective-permute-start.1
  1084.9 8.8 collective-permute-start.1
  1116.2 8.8 collective-permute-start.1
  1147.4 8.8 collective-permute-start.1
  1178.6 8.8 collective-permute-start.1
  1209.8 8.8 collective-permute-start.1
  1241.0 8.8 collective-permute-start.1
  1272.3 8.8 collective-permute-start.1
  1299.9 12.3 collective-permute-start.1
  1331.1 8.8 collective-permute-start.1
  1358.8 8.8 collective-permute-start.1
  1386.5 8.8 collective-permute-start.1
  1414.1 8.8 collective-permute-start.1
  1441.8 8.8 collective-permute-start.1
  1469.5 8.8 collective-permute-start.1
  1497.2 8.8 collective-permute-start.1
  1524.8 8.8 collective-permute-start.1
  1552.5 9.0 collective-permute-start.1
  1580.4 8.9 collective-permute-start.1
  1608.2 12.2 collective-permute-start.1
  1639.3 12.3 collective-permute-start.1
  1670.5 8.9 collective-permute-start.1
  1698.3 8.8 collective-permute-start.1
  1726.0 8.8 collective-permute-start.1
  1753.7 8.8 collective-permute-start.1
  1781.3 8.8 collective-permute-start.1
  1809.0 8.8 collective-permute-start.1
  1836.7 8.8 collective-permute-start.1
  2108.0 7.6 collective-permute-start
  (360 other events, 5348.3 us)
where the time goes:
time: 2220 us; the launch traced here: 2200 us
  starting transfers between devices  734 us (33%)
  blocking collectives  678 us (31%)
  waiting for transfers between devices  286 us (13%)
  matrix products  181 us (8%)
  other arithmetic  123 us (6%)
  loops' own time  103 us (5%)
  local copies, waits for them, and re-layouts  94.6 us (4%)
    all_gather x75, blocking collectives, tick(): patch_in = lax.all_gather(normed, 'ulysses', axis=0, tiled=True)  678 us
    ppermute x150, starting transfers between devices, passed_along(): return lax.ppermute(block, axis, route)  489 us
    all_to_all x75, starting transfers between devices, tick(): lax.all_to_all(attended_values, 'ulysses', split_axis=0, concat_axis=1, t...  245 us
    all_to_all x75, waiting for transfers between devices, tick(): lax.all_to_all(attended_values, 'ulysses', split_axis=0, concat_axis=1, t...  228 us
    another operation x1, loops' own time, shards(): result = lax.fori_loop(0, clocks, tick, start_carry)  99.3 us
    dot_general x75, matrix products, tick(): jnp.dot(latent_now.astype(jnp.bfloat16), w_in, preferred_element_type=jnp...  89 us
    dot_general x24, matrix products, project_heads(): jnp.einsum('rd,dhcn->rhcn', patch_in, weight_here, preferred_element_type...  65.6 us
    ppermute x150, waiting for transfers between devices, passed_along(): return lax.ppermute(block, axis, route)  57.7 us
  transfers between devices with their start and end apart: 225, of which 101 were waited for; matrix products, arithmetic and copies ran while one was open for 6% of the time, Pallas kernels for 0%

commit v1 on v0

v1 whole, which is shorter than its diff:
```python
import functools

import jax
import jax.numpy as jnp
from jax import lax
from jax.experimental import pallas as pl
from jax.experimental.pallas import tpu as pltpu
from jax.sharding import PartitionSpec as P

EPS = 1e-06
BF = jnp.bfloat16
F32 = jnp.float32


def contract_last(a, b):
    return lax.dot_general(a, b, (((1,), (1,)), ((), ())), preferred_element_type=F32)


def pipeline(
    dims,
    ts_ref,
    latent_ref,
    w_in_ref,
    w_out_ref,
    out_gain_ref,
    norm_gain_ref,
    modulation_ref,
    q_gain_ref,
    k_gain_ref,
    w_hbm,
    caches_ref,
    w_ref,
    gains,
    arrived,
    arrived_low,
    sent,
    sent_low,
    w_sem,
    arrived_sem,
    arrived_low_sem,
    sent_sem,
    sent_low_sem,
):
    sections, groups, steps, patches, rows, heads, hd = dims
    jobs = steps * patches
    slab = heads * hd
    width = groups * slab
    tokens = patches * rows
    section = lax.axis_index("pipe")
    member = lax.axis_index("ulysses")
    following = lax.rem(section + 1, sections)
    preceding = lax.rem(section + sections - 1, sections)
    first = section == 0
    last = section == sections - 1
    wrap = jnp.where(last, patches, 0)

    def peer(distance):
        return lax.rem(member + distance, groups)

    def w_copy(kind, head):
        column = (kind * heads + head) * hd
        return pltpu.make_async_copy(
            w_hbm.at[0, head, (1, 0, 2)[kind]],
            w_ref.at[:, column : column + hd],
            w_sem.at[kind * heads + head],
        )

    for kind in range(3):
        for head in range(heads):
            w_copy(kind, head).start()

    barrier = pltpu.get_barrier_semaphore()
    for stage in (following, preceding):
        for distance in range(groups):
            pl.semaphore_signal(
                barrier,
                inc=1,
                device_id={"pipe": stage, "ulysses": peer(distance)},
                device_id_type=pl.DeviceIdType.MESH,
            )
    pl.semaphore_wait(barrier, 2 * groups)

    caches_ref[...] = jnp.zeros_like(caches_ref)
    for step in range(steps):
        sigma = jnp.full((1, width), ts_ref[step], jnp.int32).astype(F32) / 1000.0
        gain = norm_gain_ref[...] * (1.0 + sigma * modulation_ref[...])
        for part in range(groups):
            gains[step, part] = gain[:, part * slab : (part + 1) * slab]
    for kind in range(3):
        for head in range(heads):
            w_copy(kind, head).wait()

    def send(job, distance):
        return pltpu.make_async_remote_copy(
            src_ref=sent.at[job],
            dst_ref=arrived.at[job + wrap, member],
            send_sem=sent_sem.at[job, distance],
            recv_sem=arrived_sem.at[job + wrap, member],
            device_id={"pipe": following, "ulysses": peer(distance)},
            device_id_type=pl.DeviceIdType.MESH,
        )

    def send_low(job):
        return pltpu.make_async_remote_copy(
            src_ref=sent_low.at[job],
            dst_ref=arrived_low.at[job + wrap],
            send_sem=sent_low_sem.at[job],
            recv_sem=arrived_low_sem.at[job + wrap],
            device_id={"pipe": following},
            device_id_type=pl.DeviceIdType.MESH,
        )

    def receive(job, part):
        pltpu.make_async_remote_copy(
            src_ref=sent.at[job],
            dst_ref=arrived.at[job, part],
            send_sem=sent_sem.at[job, 0],
            recv_sem=arrived_sem.at[job, part],
            device_id={"pipe": preceding},
            device_id_type=pl.DeviceIdType.MESH,
        ).wait_recv()

    def receive_low(job):
        pltpu.make_async_remote_copy(
            src_ref=sent_low.at[job],
            dst_ref=arrived_low.at[job],
            send_sem=sent_low_sem.at[job],
            recv_sem=arrived_low_sem.at[job],
            device_id={"pipe": preceding},
            device_id_type=pl.DeviceIdType.MESH,
        ).wait_recv()

    near_to_far = sorted(range(groups), key=lambda d: min(d, groups - d))

    def embed(job, patch, state):
        state = state.astype(BF)
        for distance in near_to_far:
            part = peer(distance)
            columns = pl.ds(pl.multiple_of(part * slab, slab), slab)
            x = jnp.dot(state, w_in_ref[:, columns], preferred_element_type=F32)
            high = x.astype(BF)
            arrived[job, part] = high
            if distance == 0:
                arrived_low[job] = (x - high.astype(F32)).astype(BF)

    def next_state(job, step, patch):
        square = jnp.zeros((rows, hd), F32)
        for part in range(groups):
            receive(job, part)
            x = arrived[job, part].astype(F32)
            for head in range(heads):
                piece = x[:, head * hd : (head + 1) * hd]
                square += piece * piece
        receive_low(job)
        scale = lax.rsqrt(jnp.sum(square, axis=-1, keepdims=True) / width + EPS)
        velocity = jnp.zeros((rows, latent_ref.shape[2]), F32)
        for part in range(groups):
            columns = slice(part * slab, (part + 1) * slab)
            normed = arrived[job, part].astype(F32) * scale * out_gain_ref[:, columns]
            velocity += contract_last(normed.astype(BF), w_out_ref[:, columns])
        sigma = [
            jnp.full((1, velocity.shape[1]), ts_ref[at], jnp.int32).astype(F32) / 1000.0
            for at in (0, 1)
        ]
        return latent_ref[patch] + (sigma[1] - sigma[0]) * velocity

    def run(job, _):
        step = job // patches
        patch = job - step * patches

        @pl.when(first & (step == 0))
        def _():
            embed(job, patch, latent_ref[patch])

        @pl.when(first & (step > 0))
        def _():
            embed(job, patch, next_state(job, step, patch))

        square = jnp.zeros((rows, hd), F32)
        raw = None
        for distance in near_to_far:
            part = peer(distance)

            @pl.when(jnp.logical_not(first))
            def _():
                receive(job, part)

            x = arrived[job, part].astype(F32)
            for head in range(heads):
                piece = x[:, head * hd : (head + 1) * hd]
                square += piece * piece
            h = (x * gains[step, part]).astype(BF)
            depth = pl.ds(pl.multiple_of(part * slab, slab), slab)
            term = jnp.dot(h, w_ref[depth, :], preferred_element_type=F32)
            raw = term if raw is None else raw + term
        mean_square = jnp.sum(square, axis=-1, keepdims=True) / width
        scale = lax.rsqrt(mean_square + EPS)
        eps = EPS * (mean_square + EPS)

        def of(kind, head):
            column = (kind * heads + head) * hd
            return raw[:, column : column + hd]

        def head_scale(value):
            return lax.rsqrt(jnp.mean(value * value, axis=-1, keepdims=True) + eps)

        here = pl.ds(pl.multiple_of(patch * rows, rows), rows)
        for head in range(heads):
            columns = slice(head * hd, (head + 1) * hd)
            key = of(0, head)
            key = key * head_scale(key) * k_gain_ref[...]
            caches_ref[0, 0, here, columns] = key.astype(BF)
        for head in range(heads):
            columns = slice(head * hd, (head + 1) * hd)
            caches_ref[0, 1, here, columns] = (of(2, head) * scale).astype(BF)
        limit = jnp.where(step == 0, (patch + 1) * rows, tokens)
        allowed = lax.broadcasted_iota(jnp.int32, (rows, tokens), 1) < limit
        weights = []
        for head in range(heads):
            columns = slice(head * hd, (head + 1) * hd)
            query = of(1, head)
            scores = contract_last(
                (query * q_gain_ref[...]).astype(BF), caches_ref[0, 0, :, columns]
            )
            scores = scores * (head_scale(query) * (hd**-0.5))
            weights.append(jnp.where(allowed, jnp.exp(scores), 0.0))

        @pl.when(jnp.logical_not(first))
        def _():
            receive_low(job)

        for head in range(heads):
            columns = slice(head * hd, (head + 1) * hd)
            total = jnp.sum(weights[head], axis=-1, keepdims=True)
            attended = jnp.dot(
                weights[head].astype(BF),
                caches_ref[0, 1, :, columns],
                preferred_element_type=F32,
            )
            attended = (attended / total).astype(BF).astype(F32)
            x = arrived[job, member, :, columns].astype(F32)
            x = x + arrived_low[job, :, columns].astype(F32) + attended
            high = x.astype(BF)
            sent[job, :, columns] = high
            sent_low[job, :, columns] = (x - high.astype(F32)).astype(BF)

        @pl.when(jnp.logical_not(last) | (step < steps - 1))
        def _():
            for distance in near_to_far[::-1]:
                send(job, distance).start()
            send_low(job).start()

        return 0

    lax.fori_loop(0, jobs, run, 0)

    def finish(job, _):
        @pl.when(jnp.logical_not(last) | (job < jobs - patches))
        def _():
            for distance in range(groups):
                send(job, distance).wait_send()
            send_low(job).wait_send()

        return 0

    lax.fori_loop(0, jobs, finish, 0)


def shards(latent, timesteps, w_in, w_out, out_gain, w_qkv, norm_gain, modulation, q_gain, k_gain):
    sections = lax.axis_size("pipe")
    groups = lax.axis_size("ulysses")
    patches, rows, channels = latent.shape
    steps = timesteps.shape[0]
    width = w_in.shape[1]
    heads, hd = w_qkv.shape[2], w_qkv.shape[4]
    jobs = steps * patches
    slab = heads * hd
    tokens = patches * rows
    vmem = pl.BlockSpec(memory_space=pltpu.VMEM)
    dma = pltpu.SemaphoreType.DMA
    return pl.pallas_call(
        functools.partial(pipeline, (sections, groups, steps, patches, rows, heads, hd)),
        out_shape=jax.ShapeDtypeStruct((1, 2, tokens, slab), BF),
        in_specs=[pl.BlockSpec(memory_space=pltpu.SMEM)]
        + [vmem] * 8
        + [pl.BlockSpec(memory_space=pl.ANY)],
        out_specs=vmem,
        scratch_shapes=[
            pltpu.VMEM((width, 3 * slab), BF),
            pltpu.VMEM((steps, groups, 1, slab), F32),
            pltpu.VMEM((jobs, groups, rows, slab), BF),
            pltpu.VMEM((jobs, rows, slab), BF),
            pltpu.VMEM((jobs, rows, slab), BF),
            pltpu.VMEM((jobs, rows, slab), BF),
            dma((3 * heads,)),
            dma((jobs, groups)),
            dma((jobs,)),
            dma((jobs, groups)),
            dma((jobs,)),
        ],
        compiler_params=pltpu.CompilerParams(
            collective_id=0, has_side_effects=True, vmem_limit_bytes=32 << 20
        ),
        name="pipeline",
    )(
        timesteps,
        latent,
        w_in,
        w_out.T,
        out_gain.reshape(1, width),
        norm_gain,
        modulation,
        q_gain,
        k_gain,
        jnp.transpose(w_qkv, (0, 2, 3, 1, 4)),
    )


def solution(mesh):
    placed = (
        P("rep", None, None),
        P("rep"),
        P(),
        P(),
        P(),
        P("pipe", None, "ulysses", None, None),
        P("pipe", None),
        P("pipe", None),
        P("pipe", None),
        P("pipe", None),
    )
    return jax.shard_map(
        shards,
        mesh=mesh,
        in_specs=placed,
        out_specs=P("pipe", None, "rep", "ulysses"),
        check_vma=False,
    )
```

time: 2220 us -> 350 us (0.16)
  starting transfers between devices: 734 us -> 0 us
  blocking collectives: 678 us -> 0 us
  Pallas kernels: 0 us -> 340 us
  waiting for transfers between devices: 286 us -> 0 us
  matrix products: 181 us -> 0 us
  other arithmetic: 123 us -> 0 us
  loops' own time: 103 us -> 0 us
  local copies, waits for them, and re-layouts: 94.6 us -> 9.64 us
    all_gather x75 -> x0, blocking collectives: 678 us -> none  [tick(): patch_in = lax.all_gather(normed, 'ulysses', axis=0, tiled=True)]
    ppermute x150 -> x0, starting transfers between devices: 489 us -> none  [passed_along(): return lax.ppermute(block, axis, route)]
    pallas_call x0 -> x1, Pallas kernels: none -> 340 us  [shards(): pl.pallas_call(functools.partial(pipeline, (sections, groups, steps, patc...]
    all_to_all x75 -> x0, starting transfers between devices: 245 us -> none  [tick(): lax.all_to_all(attended_values, 'ulysses', split_axis=0, concat_axis=1, t...]
    all_to_all x75 -> x0, waiting for transfers between devices: 228 us -> none  [tick(): lax.all_to_all(attended_values, 'ulysses', split_axis=0, concat_axis=1, t...]
    dot_general x222 -> x0, matrix products: 181 us -> none  [the longest x75 89 us: tick(): jnp.dot(latent_now.astype(jnp.bfloat16), w_in, preferred_element_type=jnp...]
    another operation x151 -> x0, loops' own time: 103 us -> none  [the longest x1 99.3 us: shards(): result = lax.fori_loop(0, clocks, tick, start_carry)]
    ppermute x150 -> x0, waiting for transfers between devices: 57.7 us -> none  [passed_along(): return lax.ppermute(block, axis, route)]
  transfers between devices with their start and end apart: 225 -> 0, of which waited for: 101 -> 0; matrix products, arithmetic and copies ran while one was open for 6% -> 0% of each run, Pallas kernels for 0% -> 0%
where the time goes in v1:
time: 350 us; the launch traced here: 349 us
  Pallas kernels  340 us (97%)
  local copies, waits for them, and re-layouts  9.64 us (3%)
    pallas_call x1, Pallas kernels, shards(): pl.pallas_call(functools.partial(pipeline, (sections, groups, steps, patc...  340 us
    unnamed x19, local copies, waits for them, and re-layouts  8.94 us

profile of v1, /device:TPU:505, one launch (start us, length us, event | category | flops | bytes accessed | tf_op | source)
XLA Modules:
  0.0 349.3 jit_solution(16459142822793925305)
XLA Ops:
  0.0 0.7 reshape.3.out_gain_ref
  0.7 0.0 copy-start
  0.7 2.0 copy-done
  2.7 0.0 copy-start.1
  2.7 0.9 copy-done.1
  3.6 0.0 copy-start.2
  3.6 0.9 copy-done.2
  4.6 0.0 copy-start.3
  4.6 0.9 copy-done.3
  5.5 0.0 copy-start.4
  5.5 0.7 copy-done.4
  6.2 0.0 copy-start.5
  6.2 0.7 copy-done.5
  6.9 0.0 copy-start.6
  6.9 0.7 copy-done.6
  7.5 0.0 copy-start.7
  7.5 0.7 copy-done.7
  8.2 0.0 copy-start.8
  8.2 0.7 copy-done.8
  8.8 339.6 %pipeline.1 = bf16[1,2,384,384]{3,2,1,0:T(8,128)(2,1)S(1)} custom-call(s32[2]{0:T(128)S(1)} %copy-done.6, f32[12,32,64]{2,1,0:T(8,128)S(1)} %copy-done.1, bf16[64,1536]{1,0:T(8,128)(2,1)S(1)} %copy-done.2, bf16[64,1536]{1,0:T(8,128)(2,1)S(1)} %bitcast.3, f32[1,1536]{1,0:T(1,128)S(1)} %reshape.3.out_gain_ref, f32[1,1536]{1,0:T(1,128)S(1)} %copy-done.4, ...), custom_call_target="tpu_custom_call" | custom-call | tf_op jit(solution)/shard_map/pipeline/pallas_call | solution.py:281
  348.5 0.8 copy.12
Async XLA Ops:
  0.7 2.0 copy-start
  2.7 0.9 copy-start.1
  3.6 0.9 copy-start.2
  4.6 0.9 copy-start.3
  5.5 0.7 copy-start.4
  6.2 0.7 copy-start.5
  6.9 0.7 copy-start.6
  7.5 0.7 copy-start.7
  8.2 0.7 copy-start.8

commit v2 on v1

v2 whole, which is shorter than its diff:
```python
import functools

import jax
import jax.numpy as jnp
from jax import lax
from jax.experimental import pallas as pl
from jax.experimental.pallas import tpu as pltpu
from jax.sharding import PartitionSpec as P

EPS = 1e-06
BF = jnp.bfloat16
F32 = jnp.float32


def contract_last(a, b):
    return lax.dot_general(a, b, (((1,), (1,)), ((), ())), preferred_element_type=F32)


def pipeline(
    dims,
    ts_ref,
    latent_hbm,
    w_in_hbm,
    w_out_hbm,
    out_gain_hbm,
    norm_gain_hbm,
    modulation_hbm,
    q_gain_hbm,
    k_gain_hbm,
    w_hbm,
    out_hbm,
    latent_ref,
    w_in_ref,
    w_out_ref,
    out_gain_ref,
    norm_gain_ref,
    modulation_ref,
    q_gain_ref,
    k_gain_ref,
    w_ref,
    gains,
    caches_ref,
    embedded,
    embedded_low,
    arrived,
    arrived_low,
    kept,
    sent,
    sent_low,
    edge_sem,
    w_sem,
    moved_sem,
    arrived_sem,
    low_sem,
    sent_sem,
    sent_low_sem,
    caches_sem,
    out_sem,
):
    sections, groups, steps, patches, rows, heads, hd = dims
    jobs = steps * patches
    slab = heads * hd
    width = groups * slab
    tokens = patches * rows
    section = lax.axis_index("pipe")
    member = lax.axis_index("ulysses")
    worker = lax.rem(section, 2) == 1
    helper = lax.rem(section, 2) == 0
    first = section < 2
    last = section >= sections - 2
    edge = section == 0
    following = lax.rem(section + 2, sections)
    preceding = lax.rem(section + sections - 2, sections)
    onward = jnp.where(last, 0, following)
    mesh_id = pl.DeviceIdType.MESH

    def peer(distance):
        return lax.rem(member + distance, groups)

    def greet(stage, distances):
        for distance in distances:
            pl.semaphore_signal(
                pltpu.get_barrier_semaphore(),
                inc=1,
                device_id={"pipe": stage, "ulysses": peer(distance)},
                device_id_type=mesh_id,
            )

    everyone = range(groups)

    @pl.when(helper)
    def _():
        greet(section + 1, [0])

    @pl.when(edge)
    def _():
        greet(sections - 1, everyone)

    @pl.when(worker)
    def _():
        greet(section - 1, [0])
        greet(section, everyone[1:])

    @pl.when(worker & jnp.logical_not(first))
    def _():
        greet(preceding, everyone)

    @pl.when(worker & jnp.logical_not(last))
    def _():
        greet(following, everyone)

    @pl.when(worker & last)
    def _():
        greet(0, everyone)

    met = jnp.where(
        worker,
        groups + jnp.where(first, 0, groups) + groups,
        jnp.where(edge, 1 + groups, 1),
    )

    distances = sorted(everyone, key=lambda d: min(d, groups - d))
    seen_as = {d: distances.index((groups - d) % groups) for d in everyone}

    def columns_of(at):
        return pl.ds(pl.multiple_of(peer(distances[at]) * slab, slab), slab)

    pieces = [
        (norm_gain_hbm, norm_gain_ref),
        (modulation_hbm, modulation_ref),
        (q_gain_hbm, q_gain_ref),
        (k_gain_hbm, k_gain_ref),
    ]

    def parameter(block, at):
        if at < 4:
            return pieces[at][0], pieces[at][1].at[block]
        owner, matrix = divmod(at - 4, 3 * heads)
        kind, head = divmod(matrix, heads)
        column = matrix * hd
        return (
            w_hbm.at[0, head, (1, 0, 2)[kind], columns_of(owner)],
            w_ref.at[block, owner * slab : (owner + 1) * slab, column : column + hd],
        )

    parameters = range(4 + 3 * heads * groups)

    def load(at):
        return pltpu.make_async_copy(*parameter(1, at), w_sem.at[1, at])

    def hand(at):
        source, target = parameter(0, at)
        return pltpu.make_async_remote_copy(
            src_ref=source,
            dst_ref=target,
            send_sem=moved_sem.at[at],
            recv_sem=w_sem.at[0, at],
            device_id={"pipe": section + 1},
            device_id_type=mesh_id,
        )

    def handed(at):
        source, target = parameter(0, at)
        return pltpu.make_async_copy(source, target, w_sem.at[0, at])

    def hand_back():
        return pltpu.make_async_remote_copy(
            src_ref=caches_ref.at[0],
            dst_ref=caches_ref.at[0],
            send_sem=caches_sem.at[0],
            recv_sem=caches_sem.at[1],
            device_id={"pipe": section - 1},
            device_id_type=mesh_id,
        )

    def receive(block, job, at):
        return pltpu.make_async_copy(
            sent.at[block, job], arrived.at[block, job, at], arrived_sem.at[block, job, at]
        )

    def receive_low(job):
        return pltpu.make_async_copy(sent_low.at[job], arrived_low.at[job], low_sem.at[job])

    @pl.when(helper)
    def _():
        first_only = [
            pltpu.make_async_copy(*pair, edge_sem.at[i])
            for i, pair in enumerate(
                [
                    (latent_hbm, latent_ref),
                    (w_in_hbm, w_in_ref),
                    (w_out_hbm, w_out_ref),
                    (out_gain_hbm, out_gain_ref),
                ]
            )
        ]

        @pl.when(edge)
        def _():
            for copy in first_only:
                copy.start()

        pl.semaphore_wait(pltpu.get_barrier_semaphore(), met)
        for at in parameters:
            hand(at).start()

        def hand_slab(job, at):
            return pltpu.make_async_remote_copy(
                src_ref=embedded.at[job, at],
                dst_ref=arrived.at[0, job, at],
                send_sem=sent_sem.at[0, job, at],
                recv_sem=arrived_sem.at[0, job, at],
                device_id={"pipe": section + 1},
                device_id_type=mesh_id,
            )

        def hand_low(job):
            return pltpu.make_async_remote_copy(
                src_ref=embedded_low.at[job],
                dst_ref=arrived_low.at[job],
                send_sem=sent_low_sem.at[job],
                recv_sem=low_sem.at[job],
                device_id={"pipe": section + 1},
                device_id_type=mesh_id,
            )

        def embed(job, state):
            state = state.astype(BF)
            for at in everyone:
                x = jnp.dot(state, w_in_ref[:, columns_of(at)], preferred_element_type=F32)
                high = x.astype(BF)
                embedded[job, at] = high
                if at == 0:
                    embedded_low[job] = (x - high.astype(F32)).astype(BF)
            for at in everyone:
                hand_slab(job, at).start()
            hand_low(job).start()

        def next_state(patch):
            square = jnp.zeros((rows, hd), F32)
            for at in everyone:
                receive(0, patch, at).wait()
            final = [arrived[0, patch, at].astype(F32) for at in everyone]
            for x in final:
                for head in range(heads):
                    piece = x[:, head * hd : (head + 1) * hd]
                    square += piece * piece
            scale = lax.rsqrt(jnp.sum(square, axis=-1, keepdims=True) / width + EPS)
            velocity = jnp.zeros((rows, latent_ref.shape[2]), F32)
            for at in everyone:
                normed = final[at] * scale * out_gain_ref[:, columns_of(at)]
                velocity += contract_last(normed.astype(BF), w_out_ref[:, columns_of(at)])
            sigma = [
                jnp.full((1, velocity.shape[1]), ts_ref[at], jnp.int32).astype(F32) / 1000.0
                for at in (0, 1)
            ]
            return latent_ref[patch] + (sigma[1] - sigma[0]) * velocity

        @pl.when(edge)
        def _():
            for copy in first_only:
                copy.wait()

            def start(patch, _):
                embed(patch, latent_ref[patch])
                return 0

            def again(patch, _):
                embed(patches + patch, next_state(patch))
                return 0

            def finish(job, _):
                for at in everyone:
                    hand_slab(job, at).wait_send()
                hand_low(job).wait_send()
                return 0

            lax.fori_loop(0, patches, start, 0)
            lax.fori_loop(0, patches, again, 0)
            lax.fori_loop(0, jobs, finish, 0)

        for at in parameters:
            hand(at).wait_send()
        pltpu.make_async_copy(caches_ref.at[0], caches_ref.at[0], caches_sem.at[1]).wait()
        out = pltpu.make_async_copy(caches_ref.at[0], out_hbm.at[0], out_sem)
        out.start()
        out.wait()

    @pl.when(worker)
    def _():
        for at in parameters:
            load(at).start()
        caches_ref[...] = jnp.zeros_like(caches_ref)
        pl.semaphore_wait(pltpu.get_barrier_semaphore(), met)
        for block, copy in ((0, handed), (1, load)):
            for at in range(4):
                copy(at).wait()
            for step in range(steps):
                sigma = jnp.full((1, slab), ts_ref[step], jnp.int32).astype(F32) / 1000.0
                for at in everyone:
                    gain = norm_gain_ref[block, :, columns_of(at)]
                    shift = modulation_ref[block, :, columns_of(at)]
                    gains[block, step, :, at * slab : (at + 1) * slab] = gain * (1.0 + sigma * shift)
            for at in parameters[4:]:
                copy(at).wait()

        def send(block, job, distance):
            at = seen_as[distance]
            return pltpu.make_async_remote_copy(
                src_ref=sent.at[block, job],
                dst_ref=arrived.at[1 - block, job, at],
                send_sem=sent_sem.at[block, job, distance],
                recv_sem=arrived_sem.at[1 - block, job, at],
                device_id={
                    "pipe": onward if block else section,
                    "ulysses": peer(distance),
                },
                device_id_type=mesh_id,
            )

        def send_low(job):
            return pltpu.make_async_remote_copy(
                src_ref=sent_low.at[job],
                dst_ref=arrived_low.at[job],
                send_sem=sent_low_sem.at[job],
                recv_sem=low_sem.at[job],
                device_id={"pipe": onward},
                device_id_type=mesh_id,
            )

        def run(block, step, patch):
            job = step * patches + patch
            gain = gains[block, step]
            square = jnp.zeros((rows, hd), F32)
            raw = None
            for at in everyone:
                if at or block == 0:
                    receive(block, job, at).wait()
                    x = arrived[block, job, at].astype(F32)
                else:
                    x = kept[patch]
                for head in range(heads):
                    piece = x[:, head * hd : (head + 1) * hd]
                    square += piece * piece
                x = (x * gain[:, at * slab : (at + 1) * slab]).astype(BF)
                term = jnp.dot(
                    x, w_ref[block, at * slab : (at + 1) * slab, :], preferred_element_type=F32
                )
                raw = term if raw is None else raw + term
            mean_square = jnp.sum(square, axis=-1, keepdims=True) / width
            scale = lax.rsqrt(mean_square + EPS)
            eps = EPS * (mean_square + EPS)

            def of(kind, head):
                column = (kind * heads + head) * hd
                return raw[:, column : column + hd]

            def head_scale(value):
                return lax.rsqrt(jnp.mean(value * value, axis=-1, keepdims=True) + eps)

            here = pl.ds(pl.multiple_of(patch * rows, rows), rows)
            for head in range(heads):
                columns = slice(head * hd, (head + 1) * hd)
                key = of(0, head)
                key = key * head_scale(key) * k_gain_ref[block]
                caches_ref[block, 0, here, columns] = key.astype(BF)
            for head in range(heads):
                columns = slice(head * hd, (head + 1) * hd)
                caches_ref[block, 1, here, columns] = (of(2, head) * scale).astype(BF)
            limit = jnp.where(step == 0, (patch + 1) * rows, tokens)
            allowed = lax.broadcasted_iota(jnp.int32, (rows, tokens), 1) < limit
            weights = []
            for head in range(heads):
                columns = slice(head * hd, (head + 1) * hd)
                query = of(1, head)
                scores = contract_last(
                    (query * q_gain_ref[block]).astype(BF), caches_ref[block, 0, :, columns]
                )
                scores = scores * (head_scale(query) * (hd**-0.5))
                weights.append(jnp.where(allowed, jnp.exp(scores), 0.0))
            if block == 0:
                receive_low(job).wait()
            for head in range(heads):
                columns = slice(head * hd, (head + 1) * hd)
                total = jnp.sum(weights[head], axis=-1, keepdims=True)
                attended = jnp.dot(
                    weights[head].astype(BF),
                    caches_ref[block, 1, :, columns],
                    preferred_element_type=F32,
                )
                attended = (attended / total).astype(BF).astype(F32)
                if block == 0:
                    x = arrived[0, job, 0, :, columns].astype(F32)
                    x = x + arrived_low[job, :, columns].astype(F32) + attended
                    kept[patch, :, columns] = x
                    sent[0, job, :, columns] = x.astype(BF)
                else:
                    x = kept[patch, :, columns] + attended
                    high = x.astype(BF)
                    sent[1, job, :, columns] = high
                    sent_low[job, :, columns] = (x - high.astype(F32)).astype(BF)

            if block == 0:
                for distance in distances[:0:-1]:
                    send(0, job, distance).start()
            else:

                @pl.when(jnp.logical_not(last) | (step < steps - 1))
                def _():
                    for distance in distances[::-1]:
                        send(1, job, distance).start()

                @pl.when(jnp.logical_not(last))
                def _():
                    send_low(job).start()

        turns = patches + 1

        def turn(at, _):
            step = at // turns
            patch = at - step * turns

            @pl.when(patch < patches)
            def _():
                run(0, step, patch)

            @pl.when(at == steps * turns - 1)
            def _():
                hand_back().start()

            @pl.when(patch > 0)
            def _():
                run(1, step, patch - 1)

            return 0

        lax.fori_loop(0, steps * turns, turn, 0)
        out = pltpu.make_async_copy(caches_ref.at[1], out_hbm.at[0], out_sem)
        out.start()

        def finish(job, _):
            for distance in distances[1:]:
                send(0, job, distance).wait_send()

            @pl.when(jnp.logical_not(last) | (job < jobs - patches))
            def _():
                for distance in everyone:
                    send(1, job, distance).wait_send()

            @pl.when(jnp.logical_not(last))
            def _():
                send_low(job).wait_send()

            return 0

        lax.fori_loop(0, jobs, finish, 0)
        hand_back().wait_send()
        out.wait()


def shards(latent, timesteps, w_in, w_out, out_gain, w_qkv, norm_gain, modulation, q_gain, k_gain):
    sections = lax.axis_size("pipe")
    groups = lax.axis_size("ulysses")
    patches, rows, channels = latent.shape
    steps = timesteps.shape[0]
    width = w_in.shape[1]
    heads, hd = w_qkv.shape[2], w_qkv.shape[4]
    jobs = steps * patches
    slab = heads * hd
    tokens = patches * rows
    dma = pltpu.SemaphoreType.DMA
    parameters = 4 + 3 * heads * groups
    return pl.pallas_call(
        functools.partial(pipeline, (sections, groups, steps, patches, rows, heads, hd)),
        out_shape=jax.ShapeDtypeStruct((1, 2, tokens, slab), BF),
        in_specs=[pl.BlockSpec(memory_space=pltpu.SMEM)] + [pl.BlockSpec(memory_space=pl.ANY)] * 9,
        out_specs=pl.BlockSpec(memory_space=pl.ANY),
        scratch_shapes=[
            pltpu.VMEM((patches, rows, channels), F32),
            pltpu.VMEM((channels, width), BF),
            pltpu.VMEM((channels, width), BF),
            pltpu.VMEM((1, width), F32),
            pltpu.VMEM((2, 1, width), F32),
            pltpu.VMEM((2, 1, width), F32),
            pltpu.VMEM((2, 1, hd), F32),
            pltpu.VMEM((2, 1, hd), F32),
            pltpu.VMEM((2, width, 3 * slab), BF),
            pltpu.VMEM((2, steps, 1, width), F32),
            pltpu.VMEM((2, 2, tokens, slab), BF),
            pltpu.VMEM((jobs, groups, rows, slab), BF),
            pltpu.VMEM((jobs, rows, slab), BF),
            pltpu.VMEM((2, jobs, groups, rows, slab), BF),
            pltpu.VMEM((jobs, rows, slab), BF),
            pltpu.VMEM((patches, rows, slab), F32),
            pltpu.VMEM((2, jobs, rows, slab), BF),
            pltpu.VMEM((jobs, rows, slab), BF),
            dma((4,)),
            dma((2, parameters)),
            dma((parameters,)),
            dma((2, jobs, groups)),
            dma((jobs,)),
            dma((2, jobs, groups)),
            dma((jobs,)),
            dma((2,)),
            dma,
        ],
        compiler_params=pltpu.CompilerParams(
            collective_id=0, has_side_effects=True, vmem_limit_bytes=60 << 20
        ),
        name="pipeline",
    )(
        timesteps,
        latent,
        w_in,
        w_out.T,
        out_gain.reshape(1, width),
        norm_gain,
        modulation,
        q_gain,
        k_gain,
        jnp.transpose(w_qkv, (0, 2, 3, 1, 4)),
    )


def solution(mesh):
    placed = (
        P("rep", None, None),
        P("rep"),
        P(),
        P(),
        P(),
        P("pipe", None, "ulysses", None, None),
        P("pipe", None),
        P("pipe", None),
        P("pipe", None),
        P("pipe", None),
    )
    return jax.shard_map(
        shards,
        mesh=mesh,
        in_specs=placed,
        out_specs=P("pipe", None, "rep", "ulysses"),
        check_vma=False,
    )
```

time: 350 us -> 333 us (0.951)
  Pallas kernels: 340 us -> 329 us
  local copies, waits for them, and re-layouts: 9.64 us -> 3.23 us
    pallas_call x1, Pallas kernels: 340 us -> 329 us  [shards(): pl.pallas_call(functools.partial(pipeline, (sections, groups, steps, patc...]
    unnamed x19 -> x1, local copies, waits for them, and re-layouts: 8.94 us -> 1.94 us
where the time goes in v2:
time: 333 us
  Pallas kernels  329 us (99%)
    pallas_call x1, Pallas kernels, shards(): pl.pallas_call(functools.partial(pipeline, (sections, groups, steps, patc...  329 us

profile of v2, /device:TPU:505, one launch (start us, length us, event | category | flops | bytes accessed | tf_op | source)
XLA Modules:
  0.0 332.6 jit_solution(6615033257705833799)
XLA Ops:
  0.0 1.3 reshape.3.out_gain_hbm
  1.3 329.4 %pipeline.1 = bf16[1,2,384,384]{3,2,1,0:T(8,128)(2,1)} custom-call(s32[2]{0:T(128)} %ts_ref.1, f32[12,32,64]{2,1,0:T(8,128)} %latent_hbm.1, bf16[64,1536]{1,0:T(8,128)(2,1)} %w_in_hbm.1, bf16[64,1536]{1,0:T(8,128)(2,1)} %bitcast.3, f32[1,1536]{1,0:T(1,128)} %reshape.3.out_gain_hbm, f32[1,1536]{1,0:T(1,128)} %norm_gain_hbm.1, f32[1,1536]{1,0:T(1,128)} %modulation_hbm.1, ...), custom_call_target="tpu_custom_call" | custom-call | tf_op jit(solution)/shard_map/pipeline/pallas_call | solution.py:473
  330.7 1.9 copy.12

commit v3 on v2

--- a/solution.py
+++ b/solution.py
@@ -40,8 +40,6 @@
     w_ref,
     gains,
     caches_ref,
-    embedded,
-    embedded_low,
     arrived,
     arrived_low,
     kept,
@@ -88,38 +86,35 @@
 
     everyone = range(groups)
 
-    @pl.when(helper)
+    @pl.when(helper & jnp.logical_not(edge))
     def _():
         greet(section + 1, [0])
 
     @pl.when(edge)
     def _():
         greet(sections - 1, everyone)
-
-    @pl.when(worker)
+        greet(1, everyone)
+
+    @pl.when(worker & first)
+    def _():
+        greet(0, everyone)
+
+    @pl.when(worker & jnp.logical_not(first))
     def _():
         greet(section - 1, [0])
         greet(section, everyone[1:])
-
-    @pl.when(worker & jnp.logical_not(first))
-    def _():
         greet(preceding, everyone)
 
-    @pl.when(worker & jnp.logical_not(last))
-    def _():
-        greet(following, everyone)
-
-    @pl.when(worker & last)
-    def _():
-        greet(0, everyone)
+    @pl.when(worker)
+    def _():
+        greet(onward, everyone)
 
     met = jnp.where(
-        worker,
-        groups + jnp.where(first, 0, groups) + groups,
-        jnp.where(edge, 1 + groups, 1),
+        worker, jnp.where(first, 2 * groups, 3 * groups), jnp.where(edge, 2 * groups, 1)
     )
-
-    distances = sorted(everyone, key=lambda d: min(d, groups - d))
+    leads = edge | (worker & jnp.logical_not(first))
+
+    distances = sorted(everyone, key=lambda d: (min(d, groups - d), -d))
     seen_as = {d: distances.index((groups - d) % groups) for d in everyone}
 
     def columns_of(at):
@@ -174,14 +169,25 @@
         )
 
     def receive(block, job, at):
-        return pltpu.make_async_copy(
-            sent.at[block, job], arrived.at[block, job, at], arrived_sem.at[block, job, at]
-        )
+        slot = arrived.at[block, job, at]
+        return pltpu.make_async_copy(slot, slot, arrived_sem.at[block, job, at])
 
     def receive_low(job):
         return pltpu.make_async_copy(sent_low.at[job], arrived_low.at[job], low_sem.at[job])
 
-    @pl.when(helper)
+    @pl.when(helper & jnp.logical_not(edge))
+    def _():
+        pl.semaphore_wait(pltpu.get_barrier_semaphore(), met)
+        for at in parameters:
+            hand(at).start()
+        for at in parameters:
+            hand(at).wait_send()
+        pltpu.make_async_copy(caches_ref.at[0], caches_ref.at[0], caches_sem.at[1]).wait()
+        out = pltpu.make_async_copy(caches_ref.at[0], out_hbm.at[0], out_sem)
+        out.start()
+        out.wait()
+
+    @pl.when(worker | edge)
     def _():
         first_only = [
             pltpu.make_async_copy(*pair, edge_sem.at[i])
@@ -199,100 +205,18 @@
         def _():
             for copy in first_only:
                 copy.start()
-
-        pl.semaphore_wait(pltpu.get_barrier_semaphore(), met)
-        for at in parameters:
-            hand(at).start()
-
-        def hand_slab(job, at):
-            return pltpu.make_async_remote_copy(
-                src_ref=embedded.at[job, at],
-                dst_ref=arrived.at[0, job, at],
-                send_sem=sent_sem.at[0, job, at],
-                recv_sem=arrived_sem.at[0, job, at],
-                device_id={"pipe": section + 1},
-                device_id_type=mesh_id,
-            )
-
-        def hand_low(job):
-            return pltpu.make_async_remote_copy(
-                src_ref=embedded_low.at[job],
-                dst_ref=arrived_low.at[job],
-                send_sem=sent_low_sem.at[job],
-                recv_sem=low_sem.at[job],
-                device_id={"pipe": section + 1},
-                device_id_type=mesh_id,
-            )
-
-        def embed(job, state):
-            state = state.astype(BF)
-            for at in everyone:
-                x = jnp.dot(state, w_in_ref[:, columns_of(at)], preferred_element_type=F32)
-                high = x.astype(BF)
-                embedded[job, at] = high
-                if at == 0:
-                    embedded_low[job] = (x - high.astype(F32)).astype(BF)
-            for at in everyone:
-                hand_slab(job, at).start()
-            hand_low(job).start()
-
-        def next_state(patch):
-            square = jnp.zeros((rows, hd), F32)
-            for at in everyone:
-                receive(0, patch, at).wait()
-            final = [arrived[0, patch, at].astype(F32) for at in everyone]
-            for x in final:
-                for head in range(heads):
-                    piece = x[:, head * hd : (head + 1) * hd]
-                    square += piece * piece
-            scale = lax.rsqrt(jnp.sum(square, axis=-1, keepdims=True) / width + EPS)
-            velocity = jnp.zeros((rows, latent_ref.shape[2]), F32)
-            for at in everyone:
-                normed = final[at] * scale * out_gain_ref[:, columns_of(at)]
-                velocity += contract_last(normed.astype(BF), w_out_ref[:, columns_of(at)])
-            sigma = [
-                jnp.full((1, velocity.shape[1]), ts_ref[at], jnp.int32).astype(F32) / 1000.0
-                for at in (0, 1)
-            ]
-            return latent_ref[patch] + (sigma[1] - sigma[0]) * velocity
-
-        @pl.when(edge)
-        def _():
-            for copy in first_only:
-                copy.wait()
-
-            def start(patch, _):
-                embed(patch, latent_ref[patch])
-                return 0
-
-            def again(patch, _):
-                embed(patches + patch, next_state(patch))
-                return 0
-
-            def finish(job, _):
-                for at in everyone:
-                    hand_slab(job, at).wait_send()
-                hand_low(job).wait_send()
-                return 0
-
-            lax.fori_loop(0, patches, start, 0)
-            lax.fori_loop(0, patches, again, 0)
-            lax.fori_loop(0, jobs, finish, 0)
-
-        for at in parameters:
-            hand(at).wait_send()
-        pltpu.make_async_copy(caches_ref.at[0], caches_ref.at[0], caches_sem.at[1]).wait()
-        out = pltpu.make_async_copy(caches_ref.at[0], out_hbm.at[0], out_sem)
-        out.start()
-        out.wait()
-
-    @pl.when(worker)
-    def _():
-        for at in parameters:
-            load(at).start()
+            for at in parameters:
+                handed(at).start()
+
+        @pl.when(worker)
+        def _():
+            for at in parameters:
+                load(at).start()
+
         caches_ref[...] = jnp.zeros_like(caches_ref)
         pl.semaphore_wait(pltpu.get_barrier_semaphore(), met)
-        for block, copy in ((0, handed), (1, load)):
+
+        def prepare(block, copy):
             for at in range(4):
                 copy(at).wait()
             for step in range(steps):
@@ -304,15 +228,58 @@
             for at in parameters[4:]:
                 copy(at).wait()
 
+        @pl.when(edge)
+        def _():
+            for copy in first_only:
+                copy.wait()
+
+        @pl.when(leads)
+        def _():
+            prepare(0, handed)
+
+        @pl.when(worker)
+        def _():
+            prepare(1, load)
+
+        def embed(job, state):
+            state = state.astype(BF)
+            for at in everyone:
+                x = jnp.dot(state, w_in_ref[:, columns_of(at)], preferred_element_type=F32)
+                high = x.astype(BF)
+                arrived[0, job, at] = high
+                if at == 0:
+                    arrived_low[job] = (x - high.astype(F32)).astype(BF)
+
+        def next_state(patch):
+            square = jnp.zeros((rows, hd), F32)
+            for at in everyone:
+                receive(0, jobs + patch, at).wait()
+            final = [arrived[0, jobs + patch, at].astype(F32) for at in everyone]
+            for x in final:
+                for head in range(heads):
+                    piece = x[:, head * hd : (head + 1) * hd]
+                    square += piece * piece
+            scale = lax.rsqrt(jnp.sum(square, axis=-1, keepdims=True) / width + EPS)
+            velocity = jnp.zeros((rows, latent_ref.shape[2]), F32)
+            for at in everyone:
+                normed = final[at] * scale * out_gain_ref[columns_of(at)][None, :]
+                velocity += contract_last(normed.astype(BF), w_out_ref[:, columns_of(at)])
+            sigma = [
+                jnp.full((1, velocity.shape[1]), ts_ref[at], jnp.int32).astype(F32) / 1000.0
+                for at in (0, 1)
+            ]
+            return latent_ref[patch] + (sigma[1] - sigma[0]) * velocity
+
         def send(block, job, distance):
             at = seen_as[distance]
+            slot = job + jnp.where(last, jobs, 0) if block else job
             return pltpu.make_async_remote_copy(
                 src_ref=sent.at[block, job],
-                dst_ref=arrived.at[1 - block, job, at],
+                dst_ref=arrived.at[1 - block, slot, at],
                 send_sem=sent_sem.at[block, job, distance],
-                recv_sem=arrived_sem.at[1 - block, job, at],
+                recv_sem=arrived_sem.at[1 - block, slot, at],
                 device_id={
-                    "pipe": onward if block else section,
+                    "pipe": onward if block else jnp.where(edge, 1, section),
                     "ulysses": peer(distance),
                 },
                 device_id_type=mesh_id,
@@ -324,18 +291,43 @@
                 dst_ref=arrived_low.at[job],
                 send_sem=sent_low_sem.at[job],
                 recv_sem=low_sem.at[job],
-                device_id={"pipe": onward},
+                device_id={"pipe": jnp.where(edge, 1, onward)},
                 device_id_type=mesh_id,
             )
 
         def run(block, step, patch):
             job = step * patches + patch
             gain = gains[block, step]
+            if block == 0:
+
+                @pl.when(edge & (step == 0))
+                def _():
+                    embed(job, latent_ref[patch])
+
+                @pl.when(edge & (step > 0))
+                def _():
+                    embed(job, next_state(patch))
+
+            else:
+
+                @pl.when(first)
+                def _():
+                    receive(1, job, 0).wait()
+                    receive_low(job).wait()
+                    kept[patch] = arrived[1, job, 0].astype(F32) + arrived_low[job].astype(F32)
+
             square = jnp.zeros((rows, hd), F32)
             raw = None
             for at in everyone:
+                if block == 0:
+
+                    @pl.when(jnp.logical_not(edge))
+                    def _():
+                        receive(block, job, at).wait()
+
+                elif at:
+                    receive(block, job, at).wait()
                 if at or block == 0:
-                    receive(block, job, at).wait()
                     x = arrived[block, job, at].astype(F32)
                 else:
                     x = kept[patch]
@@ -379,7 +371,11 @@
                 scores = scores * (head_scale(query) * (hd**-0.5))
                 weights.append(jnp.where(allowed, jnp.exp(scores), 0.0))
             if block == 0:
-                receive_low(job).wait()
+
+                @pl.when(jnp.logical_not(edge))
+                def _():
+                    receive_low(job).wait()
+
             for head in range(heads):
                 columns = slice(head * hd, (head + 1) * hd)
                 total = jnp.sum(weights[head], axis=-1, keepdims=True)
@@ -403,6 +399,13 @@
             if block == 0:
                 for distance in distances[:0:-1]:
                     send(0, job, distance).start()
+
+                @pl.when(edge)
+                def _():
+                    send(0, job, 0).start()
+                    sent_low[job] = (kept[patch] - sent[0, job].astype(F32)).astype(BF)
+                    send_low(job).start()
+
             else:
 
                 @pl.when(jnp.logical_not(last) | (step < steps - 1))
@@ -420,42 +423,60 @@
             step = at // turns
             patch = at - step * turns
 
-            @pl.when(patch < patches)
+            @pl.when((patch < patches) & leads)
             def _():
                 run(0, step, patch)
 
-            @pl.when(at == steps * turns - 1)
+            @pl.when((at == steps * turns - 1) & worker & jnp.logical_not(first))
             def _():
                 hand_back().start()
 
-            @pl.when(patch > 0)
+            @pl.when((patch > 0) & worker)
             def _():
                 run(1, step, patch - 1)
 
             return 0
 
         lax.fori_loop(0, steps * turns, turn, 0)
-        out = pltpu.make_async_copy(caches_ref.at[1], out_hbm.at[0], out_sem)
-        out.start()
+        def write_out(block):
+            return pltpu.make_async_copy(caches_ref.at[block], out_hbm.at[0], out_sem)
+
+        @pl.when(worker)
+        def _():
+            write_out(1).start()
+
+        @pl.when(edge)
+        def _():
+            write_out(0).start()
 
         def finish(job, _):
-            for distance in distances[1:]:
-                send(0, job, distance).wait_send()
-
-            @pl.when(jnp.logical_not(last) | (job < jobs - patches))
+            @pl.when(leads)
+            def _():
+                for distance in distances[1:]:
+                    send(0, job, distance).wait_send()
+
+            @pl.when(edge)
+            def _():
+                send(0, job, 0).wait_send()
+
+            @pl.when(worker & (jnp.logical_not(last) | (job < jobs - patches)))
             def _():
                 for distance in everyone:
                     send(1, job, distance).wait_send()
 
-            @pl.when(jnp.logical_not(last))
+            @pl.when(edge | (worker & jnp.logical_not(last)))
             def _():
                 send_low(job).wait_send()
 
             return 0
 
         lax.fori_loop(0, jobs, finish, 0)
-        hand_back().wait_send()
-        out.wait()
+
+        @pl.when(worker & jnp.logical_not(first))
+        def _():
+            hand_back().wait_send()
+
+        write_out(0).wait()
 
 
 def shards(latent, timesteps, w_in, w_out, out_gain, w_qkv, norm_gain, modulation, q_gain, k_gain):
@@ -479,7 +500,7 @@
             pltpu.VMEM((patches, rows, channels), F32),
             pltpu.VMEM((channels, width), BF),
             pltpu.VMEM((channels, width), BF),
-            pltpu.VMEM((1, width), F32),
+            pltpu.VMEM((width,), F32),
             pltpu.VMEM((2, 1, width), F32),
             pltpu.VMEM((2, 1, width), F32),
             pltpu.VMEM((2, 1, hd), F32),
@@ -487,9 +508,7 @@
             pltpu.VMEM((2, width, 3 * slab), BF),
             pltpu.VMEM((2, steps, 1, width), F32),
             pltpu.VMEM((2, 2, tokens, slab), BF),
-            pltpu.VMEM((jobs, groups, rows, slab), BF),
-            pltpu.VMEM((jobs, rows, slab), BF),
-            pltpu.VMEM((2, jobs, groups, rows, slab), BF),
+            pltpu.VMEM((2, jobs + patches, groups, rows, slab), BF),
             pltpu.VMEM((jobs, rows, slab), BF),
             pltpu.VMEM((patches, rows, slab), F32),
             pltpu.VMEM((2, jobs, rows, slab), BF),
@@ -497,7 +516,7 @@
             dma((4,)),
             dma((2, parameters)),
             dma((parameters,)),
-            dma((2, jobs, groups)),
+            dma((2, jobs + patches, groups)),
             dma((jobs,)),
             dma((2, jobs, groups)),
             dma((jobs,)),
@@ -513,7 +532,7 @@
         latent,
         w_in,
         w_out.T,
-        out_gain.reshape(1, width),
+        out_gain,
         norm_gain,
         modulation,
         q_gain,

time: 333 us -> 325 us (0.976)
  Pallas kernels: 329 us -> 323 us
    pallas_call x1, Pallas kernels: 329 us -> 323 us  [shards(): pl.pallas_call(functools.partial(pipeline, (sections, groups, steps, patc...]
where the time goes in v3:
time: 325 us
  Pallas kernels  323 us (99%)
    pallas_call x1, Pallas kernels, shards(): pl.pallas_call(functools.partial(pipeline, (sections, groups, steps, patc...  323 us

profile of v3, /device:TPU:505, one launch (start us, length us, event | category | flops | bytes accessed | tf_op | source)
XLA Modules:
  0.0 324.7 jit_solution(9810717567050353094)
XLA Ops:
  0.0 322.7 %pipeline.1 = bf16[1,2,384,384]{3,2,1,0:T(8,128)(2,1)} custom-call(s32[2]{0:T(128)} %ts_ref.1, f32[12,32,64]{2,1,0:T(8,128)} %latent_hbm.1, bf16[64,1536]{1,0:T(8,128)(2,1)} %w_in_hbm.1, bf16[64,1536]{1,0:T(8,128)(2,1)} %bitcast.3, f32[1536]{0:T(1024)} %out_gain_hbm.1, f32[1,1536]{1,0:T(1,128)} %norm_gain_hbm.1, f32[1,1536]{1,0:T(1,128)} %modulation_hbm.1, ...), custom_call_target="tpu_custom_call" | custom-call | tf_op jit(solution)/shard_map/pipeline/pallas_call | solution.py:494
  322.8 1.9 copy.12

commit v4 on v3

--- a/solution.py
+++ b/solution.py
@@ -115,6 +115,7 @@
     leads = edge | (worker & jnp.logical_not(first))
 
     distances = sorted(everyone, key=lambda d: (min(d, groups - d), -d))
+    batches = [[0, 1], list(range(2, groups))]
     seen_as = {d: distances.index((groups - d) % groups) for d in everyone}
 
     def columns_of(at):
@@ -317,26 +318,35 @@
                     kept[patch] = arrived[1, job, 0].astype(F32) + arrived_low[job].astype(F32)
 
             square = jnp.zeros((rows, hd), F32)
-            raw = None
-            for at in everyone:
+            raw, done = None, 0
+            for owners in batches:
                 if block == 0:
 
                     @pl.when(jnp.logical_not(edge))
                     def _():
-                        receive(block, job, at).wait()
-
-                elif at:
-                    receive(block, job, at).wait()
-                if at or block == 0:
-                    x = arrived[block, job, at].astype(F32)
+                        for at in owners:
+                            receive(block, job, at).wait()
+
                 else:
-                    x = kept[patch]
-                for head in range(heads):
-                    piece = x[:, head * hd : (head + 1) * hd]
-                    square += piece * piece
-                x = (x * gain[:, at * slab : (at + 1) * slab]).astype(BF)
+                    for at in owners:
+                        if at:
+                            receive(block, job, at).wait()
+                inputs = []
+                for at in owners:
+                    if at or block == 0:
+                        x = arrived[block, job, at].astype(F32)
+                    else:
+                        x = kept[patch]
+                    for head in range(heads):
+                        piece = x[:, head * hd : (head + 1) * hd]
+                        square += piece * piece
+                    inputs.append((x * gain[:, at * slab : (at + 1) * slab]).astype(BF))
+                depth = slice(done, done + len(owners) * slab)
+                done = depth.stop
                 term = jnp.dot(
-                    x, w_ref[block, at * slab : (at + 1) * slab, :], preferred_element_type=F32
+                    jnp.concatenate(inputs, axis=1) if len(inputs) > 1 else inputs[0],
+                    w_ref[block, depth, :],
+                    preferred_element_type=F32,
                 )
                 raw = term if raw is None else raw + term
             mean_square = jnp.sum(square, axis=-1, keepdims=True) / width

time: 325 us -> 313 us (0.963)
  Pallas kernels: 323 us -> 311 us
    pallas_call x1, Pallas kernels: 323 us -> 311 us  [shards(): pl.pallas_call(functools.partial(pipeline, (sections, groups, steps, patc...]
where the time goes in v4:
time: 313 us
  Pallas kernels  311 us (99%)
    pallas_call x1, Pallas kernels, shards(): pl.pallas_call(functools.partial(pipeline, (sections, groups, steps, patc...  311 us

profile of v4, /device:TPU:505, one launch (start us, length us, event | category | flops | bytes accessed | tf_op | source)
XLA Modules:
  0.0 312.9 jit_solution(13675281431473039751)
XLA Ops:
  0.0 311.0 %pipeline.1 = bf16[1,2,384,384]{3,2,1,0:T(8,128)(2,1)} custom-call(s32[2]{0:T(128)} %ts_ref.1, f32[12,32,64]{2,1,0:T(8,128)} %latent_hbm.1, bf16[64,1536]{1,0:T(8,128)(2,1)} %w_in_hbm.1, bf16[64,1536]{1,0:T(8,128)(2,1)} %bitcast.3, f32[1536]{0:T(1024)} %out_gain_hbm.1, f32[1,1536]{1,0:T(1,128)} %norm_gain_hbm.1, f32[1,1536]{1,0:T(1,128)} %modulation_hbm.1, ...), custom_call_target="tpu_custom_call" | custom-call | tf_op jit(solution)/shard_map/pipeline/pallas_call | solution.py:504
  311.0 1.9 copy.12

commit v5 on v4

--- a/solution.py
+++ b/solution.py
@@ -184,7 +184,7 @@
         for at in parameters:
             hand(at).wait_send()
         pltpu.make_async_copy(caches_ref.at[0], caches_ref.at[0], caches_sem.at[1]).wait()
-        out = pltpu.make_async_copy(caches_ref.at[0], out_hbm.at[0], out_sem)
+        out = pltpu.make_async_copy(caches_ref.at[0], out_hbm.at[0], out_sem.at[0])
         out.start()
         out.wait()
 
@@ -427,6 +427,12 @@
                 def _():
                     send_low(job).start()
 
+        def write_out(block, end):
+            lines = pl.ds(tokens - rows, rows) if end else pl.ds(0, tokens - rows)
+            return pltpu.make_async_copy(
+                caches_ref.at[block, :, lines], out_hbm.at[0, :, lines], out_sem.at[end]
+            )
+
         turns = patches + 1
 
         def turn(at, _):
@@ -441,6 +447,10 @@
             def _():
                 hand_back().start()
 
+            @pl.when((at == steps * turns - 1) & worker)
+            def _():
+                write_out(1, 0).start()
+
             @pl.when((patch > 0) & worker)
             def _():
                 run(1, step, patch - 1)
@@ -448,16 +458,14 @@
             return 0
 
         lax.fori_loop(0, steps * turns, turn, 0)
-        def write_out(block):
-            return pltpu.make_async_copy(caches_ref.at[block], out_hbm.at[0], out_sem)
-
         @pl.when(worker)
         def _():
-            write_out(1).start()
+            write_out(1, 1).start()
 
         @pl.when(edge)
         def _():
-            write_out(0).start()
+            write_out(0, 0).start()
+            write_out(0, 1).start()
 
         def finish(job, _):
             @pl.when(leads)
@@ -486,7 +494,8 @@
         def _():
             hand_back().wait_send()
 
-        write_out(0).wait()
+        write_out(0, 0).wait()
+        write_out(0, 1).wait()
 
 
 def shards(latent, timesteps, w_in, w_out, out_gain, w_qkv, norm_gain, modulation, q_gain, k_gain):
@@ -531,7 +540,7 @@
             dma((2, jobs, groups)),
             dma((jobs,)),
             dma((2,)),
-            dma,
+            dma((2,)),
         ],
         compiler_params=pltpu.CompilerParams(
             collective_id=0, has_side_effects=True, vmem_limit_bytes=60 << 20

time: 313 us -> 313 us (level)
  no operation moved by 1% of the time
where the time goes in v5:
time: 313 us
  Pallas kernels  311 us (99%)
    pallas_call x1, Pallas kernels, shards(): pl.pallas_call(functools.partial(pipeline, (sections, groups, steps, patc...  311 us

profile of v5, /device:TPU:505, one launch (start us, length us, event | category | flops | bytes accessed | tf_op | source)
XLA Modules:
  0.0 312.8 jit_solution(3364268185880377521)
XLA Ops:
  0.0 310.9 %pipeline.1 = bf16[1,2,384,384]{3,2,1,0:T(8,128)(2,1)} custom-call(s32[2]{0:T(128)} %ts_ref.1, f32[12,32,64]{2,1,0:T(8,128)} %latent_hbm.1, bf16[64,1536]{1,0:T(8,128)(2,1)} %w_in_hbm.1, bf16[64,1536]{1,0:T(8,128)(2,1)} %bitcast.3, f32[1536]{0:T(1024)} %out_gain_hbm.1, f32[1,1536]{1,0:T(1,128)} %norm_gain_hbm.1, f32[1,1536]{1,0:T(1,128)} %modulation_hbm.1, ...), custom_call_target="tpu_custom_call" | custom-call | tf_op jit(solution)/shard_map/pipeline/pallas_call | solution.py:513
  310.9 1.9 copy.12
